TPU v7x, 512 devices: a whole 4x8x8 slice. The times are simulated.
512 devices in a mesh: seq: 64 (over y, x, core), tok: 8 (over z).
Axes of the slice: x: 4, y: 8, z: 8, core: 2. Of those that a mesh axis runs over, the one named last changes fastest.
Arguments:
- queries: bfloat16 [65536, 2048], P(('seq', 'tok')), may hold values from -6 to 6
- key_vectors: bfloat16 [65536, 2048], P(('seq', 'tok')), may hold values from -6 to 6
- value_vectors: bfloat16 [65536, 2048], P(('seq', 'tok')), may hold values from -6 to 6
- grad_output: bfloat16 [65536, 2048], P(('seq', 'tok')), may hold values from -8192 to 8192
- memory: float32 [64, 16, 128, 128], P('seq', 'tok'), may hold values from -7596.0074 to 7596.0074
- normalizer: float32 [64, 16, 128], P('seq', 'tok'), may hold values from 256 to 411648
- gate_logit: float32 [16], replicated, may hold values from 4 to 7
Outputs:
- grad_queries: bfloat16 [65536, 2048], P(('seq', 'tok'))
- grad_keys: bfloat16 [65536, 2048], P(('seq', 'tok'))
- grad_values: bfloat16 [65536, 2048], P(('seq', 'tok'))
All inputs are finite; a program needn't handle non-finite values.
Results may differ from a plain program's by a relative error of at most 0.0022.
Values may be sent and summed in bfloat16 or wider, within the bound.
No kernel may reach another device: no remote copies, remote signals or barrier semaphores. Data moves between devices by JAX's collectives and lax.ppermute only.
A program may use at most 64 MiB of HBM per device.

v0:
```python
import jax
import jax.numpy as jnp
from jax import lax
from jax.sharding import PartitionSpec as P

HIGHEST = lax.Precision.HIGHEST
NEG_LARGE = -1e30


def feature_map(inputs):
    lower = jnp.exp(jnp.minimum(inputs, 0.0))
    positive = inputs > 0
    return (jnp.where(positive, inputs + 1.0, lower), jnp.where(positive, 1.0, lower))


def memory_read(query_rows, grad_rows, memory_slab, normal_vector, gate_value):
    features, slopes = feature_map(query_rows.astype(jnp.float32))
    numerator = jnp.dot(features, memory_slab, precision=HIGHEST)
    denominator = jnp.dot(features, normal_vector, precision=HIGHEST)
    scaled_grad = gate_value * grad_rows.astype(jnp.float32)
    grad_numerator = scaled_grad / denominator[:, None]
    grad_denominator = -jnp.sum(scaled_grad * numerator, axis=1) / (denominator * denominator)
    memory_grad = jnp.dot(features.T, grad_numerator, precision=HIGHEST)
    normal_grad = jnp.dot(grad_denominator, features, precision=HIGHEST)
    grad_features = (
        jnp.dot(grad_numerator, memory_slab.T, precision=HIGHEST)
        + grad_denominator[:, None] * normal_vector[None, :]
    )
    return (memory_grad, normal_grad, grad_features * slopes)


def memory_write(key_rows, value_rows, later_memory, later_normal):
    features, slopes = feature_map(key_rows.astype(jnp.float32))
    value_grad = jnp.dot(features, later_memory, precision=HIGHEST)
    feature_grad = (
        jnp.dot(value_rows.astype(jnp.float32), later_memory.T, precision=HIGHEST)
        + later_normal[None, :]
    )
    return (feature_grad * slopes, value_grad)


def attend_rows(query_rows, row_start, key_rows, value_rows, grad_rows, local_share, score_scale):
    scores = (
        jnp.einsum("qd,kd->qk", query_rows, key_rows, preferred_element_type=jnp.float32)
        * score_scale
    )
    positions = row_start + lax.broadcasted_iota(jnp.int32, scores.shape, 0)
    columns = lax.broadcasted_iota(jnp.int32, scores.shape, 1)
    scores = jnp.where(columns <= positions, scores, NEG_LARGE)
    highest = jnp.max(scores, axis=1, keepdims=True)
    exponent = jnp.exp(scores - highest)
    attention = exponent / jnp.sum(exponent, axis=1, keepdims=True)
    grad_attention = local_share * jnp.einsum(
        "qd,kd->qk", grad_rows, value_rows, preferred_element_type=jnp.float32
    )
    centre = jnp.sum(attention * grad_attention, axis=1, keepdims=True)
    grad_scores = (attention * (grad_attention - centre)).astype(jnp.bfloat16)
    grad_query = score_scale * jnp.dot(grad_scores, key_rows, preferred_element_type=jnp.float32)
    grad_key = score_scale * jnp.einsum(
        "qk,qd->kd", grad_scores, query_rows, preferred_element_type=jnp.float32
    )
    grad_value = local_share * jnp.einsum(
        "qk,qd->kd", attention.astype(jnp.bfloat16), grad_rows, preferred_element_type=jnp.float32
    )
    return (grad_query, grad_key, grad_value)


def body(queries, key_vectors, value_vectors, grad_output, memory, normalizer, gate_logit):
    groups = lax.axis_size("tok")
    head_total = gate_logit.shape[0]
    local_heads = head_total // groups
    head_size = memory.shape[-1]
    score_scale = head_size ** (-0.5)
    query_heads, key_heads, value_heads, grad_heads = (
        lax.all_to_all(queries, "tok", split_axis=1, concat_axis=0, tiled=True),
        lax.all_to_all(key_vectors, "tok", split_axis=1, concat_axis=0, tiled=True),
        lax.all_to_all(value_vectors, "tok", split_axis=1, concat_axis=0, tiled=True),
        lax.all_to_all(grad_output, "tok", split_axis=1, concat_axis=0, tiled=True),
    )
    seg_rows = query_heads.shape[0]
    gate_values = jax.nn.sigmoid(
        lax.dynamic_slice_in_dim(gate_logit, lax.axis_index("tok") * local_heads, local_heads)
    )

    def columns_of(array, head_index):
        return array[:, head_index * head_size : (head_index + 1) * head_size]

    memory_list = []
    normal_list = []
    query_memory = []
    for head_index in range(local_heads):
        memory_grad, normal_grad, query_part = memory_read(
            columns_of(query_heads, head_index),
            columns_of(grad_heads, head_index),
            memory[0, head_index],
            normalizer[0, head_index],
            gate_values[head_index],
        )
        memory_list.append(memory_grad)
        normal_list.append(normal_grad)
        query_memory.append(query_part)
    memory_grads = jnp.stack(memory_list)[None]
    normal_grads = jnp.stack(normal_list)[None]
    own_segment = lax.axis_index("seq")
    pieces = (
        lax.all_gather(memory_grads, "seq", axis=0, tiled=True),
        lax.all_gather(normal_grads, "seq", axis=0, tiled=True),
    )
    selected = (jnp.arange(pieces[0].shape[0]) > own_segment).astype(jnp.float32)
    later_memory = jnp.sum(pieces[0] * selected[:, None, None, None], axis=0, keepdims=True)
    later_normal = jnp.sum(pieces[1] * selected[:, None, None], axis=0, keepdims=True)
    block_rows = min(512, seg_rows)
    block_count = seg_rows // block_rows
    query_out = []
    key_out = []
    value_out = []
    for head_index in range(local_heads):
        query_head = columns_of(query_heads, head_index)
        key_head = columns_of(key_heads, head_index)
        value_head = columns_of(value_heads, head_index)
        grad_head = columns_of(grad_heads, head_index)
        local_share = 1.0 - gate_values[head_index]

        def block_step(carry, block_index):
            row_start = block_index * block_rows
            query_block = lax.dynamic_slice_in_dim(query_head, row_start, block_rows, 0)
            grad_block = lax.dynamic_slice_in_dim(grad_head, row_start, block_rows, 0)
            grad_query, grad_key, grad_value = attend_rows(
                query_block, row_start, key_head, value_head, grad_block, local_share, score_scale
            )
            return ((carry[0] + grad_key, carry[1] + grad_value), grad_query)

        empty = jnp.zeros((seg_rows, head_size), jnp.float32)
        (key_local, value_local), query_blocks = lax.scan(
            block_step, (empty, empty), jnp.arange(block_count)
        )
        query_local = query_blocks.reshape(seg_rows, head_size)
        key_write, value_write = memory_write(
            key_head, value_head, later_memory[0, head_index], later_normal[0, head_index]
        )
        query_out.append((query_local + query_memory[head_index]).astype(jnp.bfloat16))
        key_out.append((key_local + key_write).astype(jnp.bfloat16))
        value_out.append((value_local + value_write).astype(jnp.bfloat16))
    query_grads = jnp.concatenate(query_out, axis=1)
    key_grads = jnp.concatenate(key_out, axis=1)
    value_grads = jnp.concatenate(value_out, axis=1)
    result_q, result_k, result_v = (
        lax.all_to_all(query_grads, "tok", split_axis=0, concat_axis=1, tiled=True),
        lax.all_to_all(key_grads, "tok", split_axis=0, concat_axis=1, tiled=True),
        lax.all_to_all(value_grads, "tok", split_axis=0, concat_axis=1, tiled=True),
    )
    return (result_q, result_k, result_v)


def solution(mesh):
    in_specs = (
        P(("seq", "tok"), None),
        P(("seq", "tok"), None),
        P(("seq", "tok"), None),
        P(("seq", "tok"), None),
        P("seq", "tok", None, None),
        P("seq", "tok", None),
        P(),
    )
    out_specs = (P(("seq", "tok"), None), P(("seq", "tok"), None), P(("seq", "tok"), None))
    return jax.shard_map(body, mesh=mesh, in_specs=in_specs, out_specs=out_specs, check_vma=False)
```

profile of v0, /device:TPU:1, one launch (start us, length us, event | category | flops | bytes accessed | tf_op | source)
XLA Modules:
  0.0 267.8 jit_solution(14200388796689921154)
XLA Ops:
  7.2 2.1 copy.29
  9.3 11.0 %all-to-all-start = ((bf16[128,8,256]{0,2,1:T(8,128)(2,1)}), bf16[128,8,256]{0,2,1:T(8,128)(2,1)S(1)}, u32[]{:S(2)}, u32[]{:S(2)}) async-start(bf16[128,8,256]{0,2,1:T(8,128)(2,1)} %bitcast), calls=%async_computation | async-start | bytes 1048576 | tf_op jit(solution)/shard_map/all_to_all | solution.py:75
  21.3 17.0 %all-to-all-done = bf16[128,8,256]{0,2,1:T(8,128)(2,1)S(1)} async-done(((bf16[128,8,256]{0,2,1:T(8,128)(2,1)}), bf16[128,8,256]{0,2,1:T(8,128)(2,1)S(1)}, u32[]{:S(2)}, u32[]{:S(2)}) %all-to-all-start) | async-done | bytes 524320 | tf_op jit(solution)/shard_map/all_to_all | solution.py:75
  38.2 3.5 %all-to-all-start.2 = ((bf16[128,8,256]{0,2,1:T(8,128)(2,1)}), bf16[128,8,256]{0,2,1:T(8,128)(2,1)S(1)}, u32[]{:S(2)}, u32[]{:S(2)}) async-start(bf16[128,8,256]{0,2,1:T(8,128)(2,1)} %bitcast.5), calls=%async_computation.2 | async-start | bytes 1048576 | tf_op jit(solution)/shard_map/all_to_all | solution.py:78
  43.6 16.0 %all-to-all-done.2 = bf16[128,8,256]{0,2,1:T(8,128)(2,1)S(1)} async-done(((bf16[128,8,256]{0,2,1:T(8,128)(2,1)}), bf16[128,8,256]{0,2,1:T(8,128)(2,1)S(1)}, u32[]{:S(2)}, u32[]{:S(2)}) %all-to-all-start.2) | async-done | bytes 524320 | tf_op jit(solution)/shard_map/all_to_all | solution.py:78
  64.2 3.5 %all-to-all-start.1 = ((bf16[128,8,256]{0,2,1:T(8,128)(2,1)}), bf16[128,8,256]{0,2,1:T(8,128)(2,1)S(1)}, u32[]{:S(2)}, u32[]{:S(2)}) async-start(bf16[128,8,256]{0,2,1:T(8,128)(2,1)} %bitcast.2), calls=%async_computation.1 | async-start | bytes 1048576 | tf_op jit(solution)/shard_map/all_to_all | solution.py:76
  69.8 15.7 %all-to-all-done.1 = bf16[128,8,256]{0,2,1:T(8,128)(2,1)S(1)} async-done(((bf16[128,8,256]{0,2,1:T(8,128)(2,1)}), bf16[128,8,256]{0,2,1:T(8,128)(2,1)S(1)}, u32[]{:S(2)}, u32[]{:S(2)}) %all-to-all-start.1) | async-done | bytes 524320 | tf_op jit(solution)/shard_map/all_to_all | solution.py:76
  85.6 3.7 %all-to-all-start.3 = ((bf16[128,8,256]{2,0,1:T(8,128)(2,1)}), bf16[128,8,256]{2,0,1:T(8,128)(2,1)S(1)}, u32[]{:S(2)}, u32[]{:S(2)}) async-start(bf16[128,8,256]{2,0,1:T(8,128)(2,1)} %bitcast.177), calls=%async_computation.3 | async-start | bytes 1048576 | tf_op jit(solution)/shard_map/all_to_all | solution.py:77
  92.1 13.6 %all-to-all-done.3 = bf16[128,8,256]{2,0,1:T(8,128)(2,1)S(1)} async-done(((bf16[128,8,256]{2,0,1:T(8,128)(2,1)}), bf16[128,8,256]{2,0,1:T(8,128)(2,1)S(1)}, u32[]{:S(2)}, u32[]{:S(2)}) %all-to-all-start.3) | async-done | bytes 524320 | tf_op jit(solution)/shard_map/all_to_all | solution.py:77
  107.4 19.8 %while.30 = (s32[]{:T(128)}, f32[1024,128]{1,0:T(8,128)S(1)}, f32[1024,128]{1,0:T(8,128)}, f32[2,512,128]{2,1,0:T(8,128)}, s32[2]{0:T(128)S(1)}, /*index=5*/bf16...) while((s32[]{:T(128)}, f32[1024,128]{1,0:T(8,128)S(1)}, ...), condition=%wide.region_4.5_spmd.clone, body=%wide.region_0.4_spmd.clone.sunk | while | flops 682425344 | bytes 28863348 | solution.py:134
  110.7 2.5 fusion.219
  120.5 2.7 fusion.219
  127.2 2.1 copy.48
  131.3 19.9 %while.31 = (s32[]{:T(128)}, f32[1024,128]{1,0:T(8,128)S(1)}, f32[1024,128]{1,0:T(8,128)}, f32[2,512,128]{2,1,0:T(8,128)}, s32[2]{0:T(128)S(1)}, /*index=5*/bf16...) while((s32[]{:T(128)}, f32[1024,128]{1,0:T(8,128)S(1)}, ...), condition=%wide.region_10.11_spmd.clone, body=%wide.region_6.0_spmd.clone.sunk | while | flops 682425344 | bytes 28863348 | solution.py:134
  134.7 2.5 fusion.232
  144.5 2.7 fusion.232
  152.6 2.0 copy.54
  162.3 3.5 %all-to-all-start.4 = ((bf16[8,128,256]{1,2,0:T(8,128)(2,1)}), bf16[8,128,256]{1,2,0:T(8,128)(2,1)S(1)}, u32[]{:S(2)}, u32[]{:S(2)}) async-start(bf16[8,128,256]{1,2,0:T(8,128)(2,1)} %copy_bitcast_fusion.5), calls=%async_computation.4 | async-start | bytes 1048576 | tf_op jit(solution)/shard_map/all_to_all | solution.py:148
  167.0 39.9 %all-gather.2 = f32[64,2,128]{2,1,0:T(2,128)S(1)} all-gather(f32[1,2,128]{2,1,0:T(2,128)S(1)} %maximum_bitcast_fusion.3), channel_id=3, replica_groups=mesh['seq'=64,'tok'=8] {'seq'}, dimensions={0}, use_global_device_ids=true | all-gather | bytes 66560 | tf_op jit(solution)/shard_map/all_gather | solution.py:107
  206.9 4.3 %multiply_reduce_fusion.2 = f32[2,128,128]{2,1,0:T(8,128)S(1)} fusion(f32[64,2,128,128]{3,2,1,0:T(8,128)} %bitcast.171, f32[64]{0:T(128)S(1)} %compare_convert_fusion), kind=kLoop, calls=%fused_computation.50 | loop fusion | flops 4161536 | bytes 8519936 | tf_op jit(solution)/shard_map/reduce_sum | solution.py:110
  213.6 6.8 %all-to-all-start.6 = ((bf16[8,128,256]{1,2,0:T(8,128)(2,1)}), bf16[8,128,256]{1,2,0:T(8,128)(2,1)S(1)}, u32[]{:S(2)}, u32[]{:S(2)}) async-start(bf16[8,128,256]{1,2,0:T(8,128)(2,1)} %copy_bitcast_fusion.3), calls=%async_computation.6 | async-start | bytes 1048576 | tf_op jit(solution)/shard_map/all_to_all | solution.py:150
  224.8 13.7 %all-to-all-done.6 = bf16[8,128,256]{1,2,0:T(8,128)(2,1)S(1)} async-done(((bf16[8,128,256]{1,2,0:T(8,128)(2,1)}), bf16[8,128,256]{1,2,0:T(8,128)(2,1)S(1)}, u32[]{:S(2)}, u32[]{:S(2)}) %all-to-all-start.6) | async-done | bytes 524320 | tf_op jit(solution)/shard_map/all_to_all | solution.py:150
  238.5 3.5 %all-to-all-start.5 = ((bf16[8,128,256]{1,2,0:T(8,128)(2,1)}), bf16[8,128,256]{1,2,0:T(8,128)(2,1)S(1)}, u32[]{:S(2)}, u32[]{:S(2)}) async-start(bf16[8,128,256]{1,2,0:T(8,128)(2,1)} %copy_bitcast_fusion.4), calls=%async_computation.5 | async-start | bytes 1048576 | tf_op jit(solution)/shard_map/all_to_all | solution.py:149
  244.0 15.9 %all-to-all-done.5 = bf16[8,128,256]{1,2,0:T(8,128)(2,1)S(1)} async-done(((bf16[8,128,256]{1,2,0:T(8,128)(2,1)}), bf16[8,128,256]{1,2,0:T(8,128)(2,1)S(1)}, u32[]{:S(2)}, u32[]{:S(2)}) %all-to-all-start.5) | async-done | bytes 524320 | tf_op jit(solution)/shard_map/all_to_all | solution.py:149
  (166 shorter events, 61.1 us)
Async XLA Ops:
  7.2 13.1 %copy-start.15 = (bf16[128,2048]{1,0:T(8,128)(2,1)S(1)}, bf16[128,2048]{1,0:T(8,128)(2,1)}, u32[]{:S(2)}) copy-start(bf16[128,2048]{1,0:T(8,128)(2,1)} %param.14) | copy-start | bytes 1572868
  7.2 34.6 %copy-start.27 = (f32[16]{0:T(128)S(1)}, f32[16]{0:T(128)}, u32[]{:S(2)}) copy-start(f32[16]{0:T(128)} %param.17) | copy-start | bytes 196
  9.3 33.3 %copy-start.25 = (f32[1,2,128]{2,1,0:T(2,128)S(1)}, f32[1,2,128]{2,1,0:T(2,128)}, u32[]{:S(2)}) copy-start(f32[1,2,128]{2,1,0:T(2,128)} %param.16) | copy-start | bytes 3076
  9.3 29.0 %all-to-all-start = ((bf16[128,8,256]{0,2,1:T(8,128)(2,1)}), bf16[128,8,256]{0,2,1:T(8,128)(2,1)S(1)}, u32[]{:S(2)}, u32[]{:S(2)}) async-start(bf16[128,8,256]{0,2,1:T(8,128)(2,1)} %bitcast), calls=%async_computation | async-start | bytes 1048576 | tf_op jit(solution)/shard_map/all_to_all | solution.py:75
  38.2 21.4 %all-to-all-start.2 = ((bf16[128,8,256]{0,2,1:T(8,128)(2,1)}), bf16[128,8,256]{0,2,1:T(8,128)(2,1)S(1)}, u32[]{:S(2)}, u32[]{:S(2)}) async-start(bf16[128,8,256]{0,2,1:T(8,128)(2,1)} %bitcast.5), calls=%async_computation.2 | async-start | bytes 1048576 | tf_op jit(solution)/shard_map/all_to_all | solution.py:78
  41.7 165.1 %all-gather.5.cloned.1.call-start = ((), (), s32[]{:S(2)}) async-start(), calls=%async_computation.7 | async-start | bytes 8519680 | tf_op jit(solution)/shard_map/all_gather | solution.py:106
  42.6 47.8 %copy-start.2 = (bf16[1024,256]{0,1:T(8,128)(2,1)}, bf16[1024,256]{0,1:T(8,128)(2,1)S(1)}, u32[]{:S(2)}) copy-start(bf16[1024,256]{0,1:T(8,128)(2,1)S(1)} %copy_bitcast_fusion.2) | copy-start | bytes 1572868
  59.7 31.5 %copy-start.8 = (bf16[1024,256]{0,1:T(8,128)(2,1)}, bf16[1024,256]{0,1:T(8,128)(2,1)S(1)}, u32[]{:S(2)}) copy-start(bf16[1024,256]{0,1:T(8,128)(2,1)S(1)} %copy_bitcast_fusion) | copy-start | bytes 1572868
  61.1 7.9 %copy-start.17 = (bf16[128,2048]{1,0:T(8,128)(2,1)S(1)}, bf16[128,2048]{1,0:T(8,128)(2,1)}, u32[]{:S(2)}) copy-start(bf16[128,2048]{1,0:T(8,128)(2,1)} %param.13) | copy-start | bytes 1572868
  64.2 21.4 %all-to-all-start.1 = ((bf16[128,8,256]{0,2,1:T(8,128)(2,1)}), bf16[128,8,256]{0,2,1:T(8,128)(2,1)S(1)}, u32[]{:S(2)}, u32[]{:S(2)}) async-start(bf16[128,8,256]{0,2,1:T(8,128)(2,1)} %bitcast.2), calls=%async_computation.1 | async-start | bytes 1048576 | tf_op jit(solution)/shard_map/all_to_all | solution.py:76
  85.6 20.1 %all-to-all-start.3 = ((bf16[128,8,256]{2,0,1:T(8,128)(2,1)}), bf16[128,8,256]{2,0,1:T(8,128)(2,1)S(1)}, u32[]{:S(2)}, u32[]{:S(2)}) async-start(bf16[128,8,256]{2,0,1:T(8,128)(2,1)} %bitcast.177), calls=%async_computation.3 | async-start | bytes 1048576 | tf_op jit(solution)/shard_map/all_to_all | solution.py:77
  120.5 2.7 %copy-start.23 = (bf16[1024,128]{0,1:T(8,128)(2,1)S(1)}, bf16[1024,128]{0,1:T(8,128)(2,1)}, u32[]{:S(2)}) copy-start(bf16[1024,128]{0,1:T(8,128)(2,1)} %get-tuple-element.504) | copy-start | bytes 786436 | tf_op jit(solution)/shard_map/while
  144.5 2.7 %copy-start.21 = (bf16[1024,128]{0,1:T(8,128)(2,1)S(1)}, bf16[1024,128]{0,1:T(8,128)(2,1)}, u32[]{:S(2)}) copy-start(bf16[1024,128]{0,1:T(8,128)(2,1)} %get-tuple-element.462) | copy-start | bytes 786436 | tf_op jit(solution)/shard_map/while
  151.2 3.4 %copy-start.12 = (f32[2,512,128]{2,1,0:T(8,128)S(1)}, f32[2,512,128]{2,1,0:T(8,128)}, u32[]{:S(2)}) copy-start(f32[2,512,128]{2,1,0:T(8,128)} %get-tuple-element.112) | copy-start | bytes 1572868
  151.2 4.4 %copy-start.3 = (bf16[1024,256]{0,1:T(8,128)(2,1)S(1)}, bf16[1024,256]{0,1:T(8,128)(2,1)}, u32[]{:S(2)}) copy-start(bf16[1024,256]{0,1:T(8,128)(2,1)} %copy-done.2) | copy-start | bytes 1572868
  151.2 4.4 %copy-start.9 = (bf16[1024,256]{0,1:T(8,128)(2,1)S(1)}, bf16[1024,256]{0,1:T(8,128)(2,1)}, u32[]{:S(2)}) copy-start(bf16[1024,256]{0,1:T(8,128)(2,1)} %copy-done.8) | copy-start | bytes 1572868
  151.2 4.4 %copy-start.26 = (f32[1,2,128,128]{3,2,1,0:T(8,128)S(1)}, f32[1,2,128,128]{3,2,1,0:T(8,128)}, u32[]{:S(2)}) copy-start(f32[1,2,128,128]{3,2,1,0:T(8,128)} %param.15) | copy-start | bytes 393220
  155.7 2.9 %copy-start.20 = (f32[1024,128]{0,1:T(8,128)S(1)}, f32[1024,128]{0,1:T(8,128)}, u32[]{:S(2)}) copy-start(f32[1024,128]{0,1:T(8,128)} %copy.54) | copy-start | bytes 1572868
  162.3 51.3 %all-to-all-start.4 = ((bf16[8,128,256]{1,2,0:T(8,128)(2,1)}), bf16[8,128,256]{1,2,0:T(8,128)(2,1)S(1)}, u32[]{:S(2)}, u32[]{:S(2)}) async-start(bf16[8,128,256]{1,2,0:T(8,128)(2,1)} %copy_bitcast_fusion.5), calls=%async_computation.4 | async-start | bytes 1048576 | tf_op jit(solution)/shard_map/all_to_all | solution.py:148
  206.9 4.4 %copy-start.7 = (bf16[1024,256]{0,1:T(8,128)(2,1)S(1)}, bf16[1024,256]{0,1:T(8,128)(2,1)}, u32[]{:S(2)}) copy-start(bf16[1024,256]{0,1:T(8,128)(2,1)} %copy-done.6) | copy-start | bytes 1572868
  206.9 4.4 %copy-start.18 = (f32[1024,128]{0,1:T(8,128)S(1)}, f32[1024,128]{0,1:T(8,128)}, u32[]{:S(2)}) copy-start(f32[1024,128]{0,1:T(8,128)} %copy.48) | copy-start | bytes 1572868
  212.7 9.1 %copy-start.5 = (bf16[128,8,256]{2,0,1:T(8,128)(2,1)S(1)}, bf16[128,8,256]{2,0,1:T(8,128)(2,1)}, u32[]{:S(2)}) copy-start(bf16[128,8,256]{2,0,1:T(8,128)(2,1)} %copy-done.4) | copy-start | bytes 1572868
  213.6 24.9 %all-to-all-start.6 = ((bf16[8,128,256]{1,2,0:T(8,128)(2,1)}), bf16[8,128,256]{1,2,0:T(8,128)(2,1)S(1)}, u32[]{:S(2)}, u32[]{:S(2)}) async-start(bf16[8,128,256]{1,2,0:T(8,128)(2,1)} %copy_bitcast_fusion.3), calls=%async_computation.6 | async-start | bytes 1048576 | tf_op jit(solution)/shard_map/all_to_all | solution.py:150
  238.5 21.4 %all-to-all-start.5 = ((bf16[8,128,256]{1,2,0:T(8,128)(2,1)}), bf16[8,128,256]{1,2,0:T(8,128)(2,1)S(1)}, u32[]{:S(2)}, u32[]{:S(2)}) async-start(bf16[8,128,256]{1,2,0:T(8,128)(2,1)} %copy_bitcast_fusion.4), calls=%async_computation.5 | async-start | bytes 1048576 | tf_op jit(solution)/shard_map/all_to_all | solution.py:149
  (22 other events, 33.0 us)
Sparse Core Ops, SparseCore 0:
  63.3 84.5 all-gather.4
where the time goes:
time: 269 us; the launch traced here: 268 us
  waiting for transfers between devices  91.9 us (34%)
  blocking collectives  39.9 us (15%)
  matrix products  39.2 us (15%)
  starting transfers between devices  35.5 us (13%)
  local copies, waits for them, and re-layouts  30.3 us (11%)
  between operations  15.7 us (6%)
  other arithmetic  12.3 us (5%)
  loops' own time  2.88 us (1%)
    all_gather x1, blocking collectives, body(): lax.all_gather(normal_grads, 'seq', axis=0, tiled=True)  39.9 us
    all_to_all x1, waiting for transfers between devices, body(): lax.all_to_all(queries, 'tok', split_axis=1, concat_axis=0, tiled=True)  17 us
    all_to_all x1, waiting for transfers between devices, body(): lax.all_to_all(grad_output, 'tok', split_axis=1, concat_axis=0, tiled=True)  16 us
    all_to_all x1, waiting for transfers between devices, body(): lax.all_to_all(key_grads, 'tok', split_axis=0, concat_axis=1, tiled=True)  15.9 us
    all_to_all x1, waiting for transfers between devices, body(): lax.all_to_all(key_vectors, 'tok', split_axis=1, concat_axis=0, tiled=True)  15.7 us
    all_to_all x1, waiting for transfers between devices, body(): lax.all_to_all(value_grads, 'tok', split_axis=0, concat_axis=1, tiled=True)  13.7 us
    all_to_all x1, waiting for transfers between devices, body(): lax.all_to_all(value_vectors, 'tok', split_axis=1, concat_axis=0, tiled=T...  13.6 us
    all_to_all x1, starting transfers between devices, body(): lax.all_to_all(queries, 'tok', split_axis=1, concat_axis=0, tiled=True)  11 us
  transfers between devices with their start and end apart: 8, of which 6 were waited for; matrix products, arithmetic and copies ran while one was open for 26% of the time, Pallas kernels for 0%

commit v1 on v0

--- a/solution.py
+++ b/solution.py
@@ -5,6 +5,22 @@
 
 HIGHEST = lax.Precision.HIGHEST
 NEG_LARGE = -1e30
+
+
+def pairwise_exchange(x, axis, split, join):
+    ways, here = (lax.axis_size(axis), lax.axis_index(axis))
+    width = x.shape[split] // ways
+    shape = list(x.shape)
+    shape[split] = width
+    height = shape[join]
+    shape[join] = height * ways
+    full = jnp.zeros(shape, x.dtype)
+    for mask in range(ways):
+        part = lax.dynamic_slice_in_dim(x, (here ^ mask) * width, width, axis=split)
+        if mask:
+            part = lax.ppermute(part, axis, [(d, d ^ mask) for d in range(ways)])
+        full = lax.dynamic_update_slice_in_dim(full, part, (here ^ mask) * height, axis=join)
+    return full
 
 
 def feature_map(inputs):
@@ -73,7 +89,7 @@
     score_scale = head_size ** (-0.5)
     query_heads, key_heads, value_heads, grad_heads = (
         lax.all_to_all(queries, "tok", split_axis=1, concat_axis=0, tiled=True),
-        lax.all_to_all(key_vectors, "tok", split_axis=1, concat_axis=0, tiled=True),
+        pairwise_exchange(key_vectors, "tok", 1, 0),
         lax.all_to_all(value_vectors, "tok", split_axis=1, concat_axis=0, tiled=True),
         lax.all_to_all(grad_output, "tok", split_axis=1, concat_axis=0, tiled=True),
     )

time: 269 us -> 276 us (1.026)
  starting transfers between devices: 35.5 us -> 58.2 us
  waiting for transfers between devices: 91.9 us -> 73.1 us
  matrix products: 39.2 us -> 45.8 us
  local copies, waits for them, and re-layouts: 30.3 us -> 25.5 us
    ppermute x0 -> x7, starting transfers between devices: none -> 24.8 us  [pairwise_exchange(): part = lax.ppermute(part, axis, [(d, d ^ mask) for d in range(ways)])]
    all_to_all x1 -> x0, waiting for transfers between devices: 15.7 us -> none  [body(): lax.all_to_all(key_vectors, 'tok', split_axis=1, concat_axis=0, tiled=True)]
    all_to_all x1, waiting for transfers between devices: 13.6 us -> 0.01 us  [body(): lax.all_to_all(value_vectors, 'tok', split_axis=1, concat_axis=0, tiled=T...]
    ppermute x0 -> x7, waiting for transfers between devices: none -> 9.1 us  [pairwise_exchange(): part = lax.ppermute(part, axis, [(d, d ^ mask) for d in range(ways)])]
    dot_general x4, matrix products: 2.44 us -> 9.42 us  [attend_rows(): jnp.einsum('qk,qd->kd', grad_scores, query_rows, preferred_element_type=j...]
    dot_general x4, matrix products: 10.3 us -> 5.38 us  [attend_rows(): jnp.einsum('qk,qd->kd', attention.astype(jnp.bfloat16), grad_rows, prefer...]
    while x4, local copies, waits for them, and re-layouts: 4.61 us -> 0.79 us  [body(): lax.scan(block_step, (empty, empty), jnp.arange(block_count))]
    all_to_all x1 -> x0, starting transfers between devices: 3.49 us -> none  [body(): lax.all_to_all(key_vectors, 'tok', split_axis=1, concat_axis=0, tiled=True)]
  transfers between devices with their start and end apart: 8 -> 14, of which waited for: 6 -> 6; matrix products, arithmetic and copies ran while one was open for 26% -> 26% of each run, Pallas kernels for 0% -> 0%
where the time goes in v1:
time: 276 us; the launch traced here: 275 us
  waiting for transfers between devices  73.1 us (26%)
  starting transfers between devices  58.2 us (21%)
  matrix products  45.8 us (17%)
  blocking collectives  40.9 us (15%)
  local copies, waits for them, and re-layouts  25.5 us (9%)
  between operations  16.1 us (6%)
  other arithmetic  12.3 us (4%)
  loops' own time  3 us (1%)
    all_gather x1, blocking collectives, body(): lax.all_gather(normal_grads, 'seq', axis=0, tiled=True)  40.9 us
    ppermute x7, starting transfers between devices, pairwise_exchange(): part = lax.ppermute(part, axis, [(d, d ^ mask) for d in range(ways)])  24.8 us
    all_to_all x1, waiting for transfers between devices, body(): lax.all_to_all(queries, 'tok', split_axis=1, concat_axis=0, tiled=True)  17 us
    all_to_all x1, waiting for transfers between devices, body(): lax.all_to_all(grad_output, 'tok', split_axis=1, concat_axis=0, tiled=True)  16 us
    all_to_all x1, waiting for transfers between devices, body(): lax.all_to_all(value_grads, 'tok', split_axis=0, concat_axis=1, tiled=True)  15.9 us
    all_to_all x1, waiting for transfers between devices, body(): lax.all_to_all(key_grads, 'tok', split_axis=0, concat_axis=1, tiled=True)  15.2 us
    all_to_all x1, starting transfers between devices, body(): lax.all_to_all(queries, 'tok', split_axis=1, concat_axis=0, tiled=True)  11 us
    dot_general x4, matrix products, attend_rows(): jnp.einsum('qk,qd->kd', grad_scores, query_rows, preferred_element_type=j...  9.42 us
  transfers between devices with their start and end apart: 14, of which 6 were waited for; matrix products, arithmetic and copies ran while one was open for 26% of the time, Pallas kernels for 0%

profile of v1, /device:TPU:1, one launch (start us, length us, event | category | flops | bytes accessed | tf_op | source)
XLA Modules:
  0.0 275.0 jit_solution(4312582488180875248)
XLA Ops:
  9.3 11.0 %all-to-all-start = ((bf16[128,8,256]{0,2,1:T(8,128)(2,1)}), bf16[128,8,256]{0,2,1:T(8,128)(2,1)S(1)}, u32[]{:S(2)}, u32[]{:S(2)}) async-start(bf16[128,8,256]{0,2,1:T(8,128)(2,1)} %bitcast), calls=%async_computation | async-start | bytes 1048576 | tf_op jit(solution)/shard_map/all_to_all | solution.py:91
  21.3 17.0 %all-to-all-done = bf16[128,8,256]{0,2,1:T(8,128)(2,1)S(1)} async-done(((bf16[128,8,256]{0,2,1:T(8,128)(2,1)}), bf16[128,8,256]{0,2,1:T(8,128)(2,1)S(1)}, u32[]{:S(2)}, u32[]{:S(2)}) %all-to-all-start) | async-done | bytes 524320 | tf_op jit(solution)/shard_map/all_to_all | solution.py:91
  38.2 3.5 %all-to-all-start.1 = ((bf16[128,8,256]{0,2,1:T(8,128)(2,1)}), bf16[128,8,256]{0,2,1:T(8,128)(2,1)S(1)}, u32[]{:S(2)}, u32[]{:S(2)}) async-start(bf16[128,8,256]{0,2,1:T(8,128)(2,1)} %bitcast.3), calls=%async_computation.1 | async-start | bytes 1048576 | tf_op jit(solution)/shard_map/all_to_all | solution.py:94
  43.6 16.0 %all-to-all-done.1 = bf16[128,8,256]{0,2,1:T(8,128)(2,1)S(1)} async-done(((bf16[128,8,256]{0,2,1:T(8,128)(2,1)}), bf16[128,8,256]{0,2,1:T(8,128)(2,1)S(1)}, u32[]{:S(2)}, u32[]{:S(2)}) %all-to-all-start.1) | async-done | bytes 524320 | tf_op jit(solution)/shard_map/all_to_all | solution.py:94
  67.6 5.4 %collective-permute-start.2 = (bf16[128,256]{0,1:T(8,128)(2,1)S(1)}, bf16[128,256]{0,1:T(8,128)(2,1)S(1)}, u32[]{:S(2)}, u32[]{:S(2)}) collective-permute-start(bf16[128,256]{0,1:T(8,128)(2,1)S(1)} %copy.76), channel_id=1, source_target_pairs={{0,3},{1,2},{2,1},{3,0},{4,7},{5,6},{6,5},{7,4},{8,11},{9,10},{10,... | collective-permute-start | bytes 196616 | tf_op jit(solution)/shard_map/ppermute | solution.py:21
  75.2 5.2 %collective-permute-start.4 = (bf16[128,256]{0,1:T(8,128)(2,1)S(1)}, bf16[128,256]{0,1:T(8,128)(2,1)S(1)}, u32[]{:S(2)}, u32[]{:S(2)}) collective-permute-start(bf16[128,256]{0,1:T(8,128)(2,1)S(1)} %copy.78), channel_id=1, source_target_pairs={{0,5},{1,4},{2,7},{3,6},{4,1},{5,0},{6,3},{7,2},{8,13},{9,12},{10,... | collective-permute-start | bytes 196616 | tf_op jit(solution)/shard_map/ppermute | solution.py:21
  81.3 3.6 %all-to-all-start.2 = ((bf16[128,8,256]{2,0,1:T(8,128)(2,1)}), bf16[128,8,256]{2,0,1:T(8,128)(2,1)S(1)}, u32[]{:S(2)}, u32[]{:S(2)}) async-start(bf16[128,8,256]{2,0,1:T(8,128)(2,1)} %bitcast.127), calls=%async_computation.2 | async-start | bytes 1048576 | tf_op jit(solution)/shard_map/all_to_all | solution.py:93
  86.8 5.4 %collective-permute-start.5 = (bf16[128,256]{0,1:T(8,128)(2,1)S(1)}, bf16[128,256]{0,1:T(8,128)(2,1)S(1)}, u32[]{:S(2)}, u32[]{:S(2)}) collective-permute-start(bf16[128,256]{0,1:T(8,128)(2,1)S(1)} %copy.79), channel_id=1, source_target_pairs={{0,6},{1,7},{2,4},{3,5},{4,2},{5,3},{6,0},{7,1},{8,14},{9,15},{10,... | collective-permute-start | bytes 196616 | tf_op jit(solution)/shard_map/ppermute | solution.py:21
  92.3 3.0 %collective-permute-start.6 = (bf16[128,256]{0,1:T(8,128)(2,1)S(1)}, bf16[128,256]{0,1:T(8,128)(2,1)S(1)}, u32[]{:S(2)}, u32[]{:S(2)}) collective-permute-start(bf16[128,256]{0,1:T(8,128)(2,1)S(1)} %copy.80), channel_id=1, source_target_pairs={{0,7},{1,6},{2,5},{3,4},{4,3},{5,2},{6,1},{7,0},{8,15},{9,14},{10,... | collective-permute-start | bytes 196616 | tf_op jit(solution)/shard_map/ppermute | solution.py:21
  95.4 4.7 %collective-permute-done.5 = bf16[128,256]{0,1:T(8,128)(2,1)S(1)} collective-permute-done((bf16[128,256]{0,1:T(8,128)(2,1)S(1)}, bf16[128,256]{0,1:T(8,128)(2,1)S(1)}, u32[]{:S(2)}, u32[]{:S(2)}) %collective-permute-start.5) | collective-permute-done | bytes 65568 | tf_op jit(solution)/shard_map/ppermute | solution.py:21
  100.1 4.4 %collective-permute-done.6 = bf16[128,256]{0,1:T(8,128)(2,1)S(1)} collective-permute-done((bf16[128,256]{0,1:T(8,128)(2,1)S(1)}, bf16[128,256]{0,1:T(8,128)(2,1)S(1)}, u32[]{:S(2)}, u32[]{:S(2)}) %collective-permute-start.6) | collective-permute-done | bytes 65568 | tf_op jit(solution)/shard_map/ppermute | solution.py:21
  109.9 25.3 %while.31 = (s32[]{:T(128)}, f32[1024,128]{1,0:T(8,128)}, f32[1024,128]{1,0:T(8,128)}, f32[2,512,128]{2,1,0:T(8,128)}, s32[2]{0:T(128)S(1)}, /*index=5*/bf16[102...) while((s32[]{:T(128)}, f32[1024,128]{1,0:T(8,128)}, ...), condition=%wide.region_10.11_spmd.clone, body=%wide.region_6.0_spmd.clone.sunk | while | flops 682425344 | bytes 29912412 | solution.py:150
  128.4 2.5 fusion.230
  138.0 19.8 %while.30 = (s32[]{:T(128)}, f32[1024,128]{1,0:T(8,128)}, f32[1024,128]{1,0:T(8,128)}, f32[2,512,128]{2,1,0:T(8,128)}, s32[2]{0:T(128)S(1)}, /*index=5*/bf16[102...) while((s32[]{:T(128)}, f32[1024,128]{1,0:T(8,128)}, ...), condition=%wide.region_4.5_spmd.clone, body=%wide.region_0.4_spmd.clone.sunk | while | flops 682425344 | bytes 33057208 | solution.py:150
  143.3 2.2 fusion.217
  153.1 2.4 fusion.217
  159.2 2.5 fusion.45
  167.0 4.9 %all-to-all-start.3 = ((bf16[8,128,256]{1,2,0:T(8,128)(2,1)}), bf16[8,128,256]{1,2,0:T(8,128)(2,1)S(1)}, u32[]{:S(2)}, u32[]{:S(2)}) async-start(bf16[8,128,256]{1,2,0:T(8,128)(2,1)} %copy_bitcast_fusion.4), calls=%async_computation.3 | async-start | bytes 1048576 | tf_op jit(solution)/shard_map/all_to_all | solution.py:164
  173.4 40.9 %all-gather.2 = f32[64,2,128]{2,1,0:T(2,128)S(1)} all-gather(f32[1,2,128]{2,1,0:T(2,128)S(1)} %maximum_bitcast_fusion.3), channel_id=3, replica_groups=mesh['seq'=64,'tok'=8] {'seq'}, dimensions={0}, use_global_device_ids=true | all-gather | bytes 66560 | tf_op jit(solution)/shard_map/all_gather | solution.py:123
  214.6 4.3 %multiply_reduce_fusion.2 = f32[2,128,128]{2,1,0:T(8,128)S(1)} fusion(f32[64,2,128,128]{3,2,1,0:T(8,128)} %bitcast.156, f32[64]{0:T(128)S(1)} %compare_convert_fusion), kind=kLoop, calls=%fused_computation.50 | loop fusion | flops 4161536 | bytes 8519936 | tf_op jit(solution)/shard_map/reduce_sum | solution.py:126
  220.8 6.9 %all-to-all-start.4 = ((bf16[8,128,256]{1,2,0:T(8,128)(2,1)}), bf16[8,128,256]{1,2,0:T(8,128)(2,1)S(1)}, u32[]{:S(2)}, u32[]{:S(2)}) async-start(bf16[8,128,256]{1,2,0:T(8,128)(2,1)} %copy_bitcast_fusion.3), calls=%async_computation.4 | async-start | bytes 1048576 | tf_op jit(solution)/shard_map/all_to_all | solution.py:165
  230.6 15.2 %all-to-all-done.4 = bf16[8,128,256]{1,2,0:T(8,128)(2,1)S(1)} async-done(((bf16[8,128,256]{1,2,0:T(8,128)(2,1)}), bf16[8,128,256]{1,2,0:T(8,128)(2,1)S(1)}, u32[]{:S(2)}, u32[]{:S(2)}) %all-to-all-start.4) | async-done | bytes 524320 | tf_op jit(solution)/shard_map/all_to_all | solution.py:165
  245.8 3.5 %all-to-all-start.5 = ((bf16[8,128,256]{1,2,0:T(8,128)(2,1)}), bf16[8,128,256]{1,2,0:T(8,128)(2,1)S(1)}, u32[]{:S(2)}, u32[]{:S(2)}) async-start(bf16[8,128,256]{1,2,0:T(8,128)(2,1)} %copy_bitcast_fusion.2), calls=%async_computation.5 | async-start | bytes 1048576 | tf_op jit(solution)/shard_map/all_to_all | solution.py:166
  251.3 15.9 %all-to-all-done.5 = bf16[8,128,256]{1,2,0:T(8,128)(2,1)S(1)} async-done(((bf16[8,128,256]{1,2,0:T(8,128)(2,1)}), bf16[8,128,256]{1,2,0:T(8,128)(2,1)S(1)}, u32[]{:S(2)}, u32[]{:S(2)}) %all-to-all-start.5) | async-done | bytes 524320 | tf_op jit(solution)/shard_map/all_to_all | solution.py:166
  (200 shorter events, 75.4 us)
Async XLA Ops:
  7.2 13.1 %copy-start.14 = (bf16[128,2048]{1,0:T(8,128)(2,1)S(1)}, bf16[128,2048]{1,0:T(8,128)(2,1)}, u32[]{:S(2)}) copy-start(bf16[128,2048]{1,0:T(8,128)(2,1)} %param.14) | copy-start | bytes 1572868
  7.2 34.6 %copy-start.29 = (f32[16]{0:T(128)S(1)}, f32[16]{0:T(128)}, u32[]{:S(2)}) copy-start(f32[16]{0:T(128)} %param.17) | copy-start | bytes 196
  9.3 33.3 %copy-start.27 = (f32[1,2,128]{2,1,0:T(2,128)S(1)}, f32[1,2,128]{2,1,0:T(2,128)}, u32[]{:S(2)}) copy-start(f32[1,2,128]{2,1,0:T(2,128)} %param.16) | copy-start | bytes 3076
  9.3 29.0 %all-to-all-start = ((bf16[128,8,256]{0,2,1:T(8,128)(2,1)}), bf16[128,8,256]{0,2,1:T(8,128)(2,1)S(1)}, u32[]{:S(2)}, u32[]{:S(2)}) async-start(bf16[128,8,256]{0,2,1:T(8,128)(2,1)} %bitcast), calls=%async_computation | async-start | bytes 1048576 | tf_op jit(solution)/shard_map/all_to_all | solution.py:91
  38.2 21.4 %all-to-all-start.1 = ((bf16[128,8,256]{0,2,1:T(8,128)(2,1)}), bf16[128,8,256]{0,2,1:T(8,128)(2,1)S(1)}, u32[]{:S(2)}, u32[]{:S(2)}) async-start(bf16[128,8,256]{0,2,1:T(8,128)(2,1)} %bitcast.3), calls=%async_computation.1 | async-start | bytes 1048576 | tf_op jit(solution)/shard_map/all_to_all | solution.py:94
  41.7 172.8 %all-gather.5.cloned.1.call-start = ((), (), s32[]{:S(2)}) async-start(), calls=%async_computation.6 | async-start | bytes 8519680 | tf_op jit(solution)/shard_map/all_gather | solution.py:122
  42.6 63.7 %copy-start.2 = (bf16[1024,256]{0,1:T(8,128)(2,1)}, bf16[1024,256]{0,1:T(8,128)(2,1)S(1)}, u32[]{:S(2)}) copy-start(bf16[1024,256]{0,1:T(8,128)(2,1)S(1)} %copy_bitcast_fusion.1) | copy-start | bytes 1572868
  59.7 47.6 %copy-start.4 = (bf16[1024,256]{0,1:T(8,128)(2,1)}, bf16[1024,256]{0,1:T(8,128)(2,1)S(1)}, u32[]{:S(2)}) copy-start(bf16[1024,256]{0,1:T(8,128)(2,1)S(1)} %copy_bitcast_fusion) | copy-start | bytes 1572868
  61.1 19.3 %copy-start.16 = (bf16[128,2048]{1,0:T(8,128)(2,1)S(1)}, bf16[128,2048]{1,0:T(8,128)(2,1)}, u32[]{:S(2)}) copy-start(bf16[128,2048]{1,0:T(8,128)(2,1)} %param.13) | copy-start | bytes 1572868
  63.5 23.3 %collective-permute-start = (bf16[128,256]{0,1:T(8,128)(2,1)S(1)}, bf16[128,256]{0,1:T(8,128)(2,1)S(1)}, u32[]{:S(2)}, u32[]{:S(2)}) collective-permute-start(bf16[128,256]{0,1:T(8,128)(2,1)S(1)} %copy.74), channel_id=1, source_target_pairs={{0,1},{1,0},{2,3},{3,2},{4,5},{5,4},{6,7},{7,6},{8,9},{9,8},{10,11... | collective-permute-start | bytes 196616 | tf_op jit(solution)/shard_map/ppermute | solution.py:21
  65.6 26.7 %collective-permute-start.1 = (bf16[128,256]{0,1:T(8,128)(2,1)S(1)}, bf16[128,256]{0,1:T(8,128)(2,1)S(1)}, u32[]{:S(2)}, u32[]{:S(2)}) collective-permute-start(bf16[128,256]{0,1:T(8,128)(2,1)S(1)} %copy.75), channel_id=1, source_target_pairs={{0,2},{1,3},{2,0},{3,1},{4,6},{5,7},{6,4},{7,5},{8,10},{9,11},{10,... | collective-permute-start | bytes 196616 | tf_op jit(solution)/shard_map/ppermute | solution.py:21
  67.6 27.7 %collective-permute-start.2 = (bf16[128,256]{0,1:T(8,128)(2,1)S(1)}, bf16[128,256]{0,1:T(8,128)(2,1)S(1)}, u32[]{:S(2)}, u32[]{:S(2)}) collective-permute-start(bf16[128,256]{0,1:T(8,128)(2,1)S(1)} %copy.76), channel_id=1, source_target_pairs={{0,3},{1,2},{2,1},{3,0},{4,7},{5,6},{6,5},{7,4},{8,11},{9,10},{10,... | collective-permute-start | bytes 196616 | tf_op jit(solution)/shard_map/ppermute | solution.py:21
  73.2 22.1 %collective-permute-start.3 = (bf16[128,256]{0,1:T(8,128)(2,1)S(1)}, bf16[128,256]{0,1:T(8,128)(2,1)S(1)}, u32[]{:S(2)}, u32[]{:S(2)}) collective-permute-start(bf16[128,256]{0,1:T(8,128)(2,1)S(1)} %copy.77), channel_id=1, source_target_pairs={{0,4},{1,5},{2,6},{3,7},{4,0},{5,1},{6,2},{7,3},{8,12},{9,13},{10,... | collective-permute-start | bytes 196616 | tf_op jit(solution)/shard_map/ppermute | solution.py:21
  75.2 20.1 %collective-permute-start.4 = (bf16[128,256]{0,1:T(8,128)(2,1)S(1)}, bf16[128,256]{0,1:T(8,128)(2,1)S(1)}, u32[]{:S(2)}, u32[]{:S(2)}) collective-permute-start(bf16[128,256]{0,1:T(8,128)(2,1)S(1)} %copy.78), channel_id=1, source_target_pairs={{0,5},{1,4},{2,7},{3,6},{4,1},{5,0},{6,3},{7,2},{8,13},{9,12},{10,... | collective-permute-start | bytes 196616 | tf_op jit(solution)/shard_map/ppermute | solution.py:21
  81.3 26.9 %all-to-all-start.2 = ((bf16[128,8,256]{2,0,1:T(8,128)(2,1)}), bf16[128,8,256]{2,0,1:T(8,128)(2,1)S(1)}, u32[]{:S(2)}, u32[]{:S(2)}) async-start(bf16[128,8,256]{2,0,1:T(8,128)(2,1)} %bitcast.127), calls=%async_computation.2 | async-start | bytes 1048576 | tf_op jit(solution)/shard_map/all_to_all | solution.py:93
  86.8 13.3 %collective-permute-start.5 = (bf16[128,256]{0,1:T(8,128)(2,1)S(1)}, bf16[128,256]{0,1:T(8,128)(2,1)S(1)}, u32[]{:S(2)}, u32[]{:S(2)}) collective-permute-start(bf16[128,256]{0,1:T(8,128)(2,1)S(1)} %copy.79), channel_id=1, source_target_pairs={{0,6},{1,7},{2,4},{3,5},{4,2},{5,3},{6,0},{7,1},{8,14},{9,15},{10,... | collective-permute-start | bytes 196616 | tf_op jit(solution)/shard_map/ppermute | solution.py:21
  92.3 12.2 %collective-permute-start.6 = (bf16[128,256]{0,1:T(8,128)(2,1)S(1)}, bf16[128,256]{0,1:T(8,128)(2,1)S(1)}, u32[]{:S(2)}, u32[]{:S(2)}) collective-permute-start(bf16[128,256]{0,1:T(8,128)(2,1)S(1)} %copy.80), channel_id=1, source_target_pairs={{0,7},{1,6},{2,5},{3,4},{4,3},{5,2},{6,1},{7,0},{8,15},{9,14},{10,... | collective-permute-start | bytes 196616 | tf_op jit(solution)/shard_map/ppermute | solution.py:21
  164.6 7.3 %copy-start.1 = (f32[1024,128]{1,0:T(8,128)S(1)}, f32[1024,128]{1,0:T(8,128)}, u32[]{:S(2)}) copy-start(f32[1024,128]{1,0:T(8,128)} %get-tuple-element.114) | copy-start | bytes 1572868
  166.1 6.0 %copy-start = (f32[1024,128]{1,0:T(8,128)S(1)}, f32[1024,128]{1,0:T(8,128)}, u32[]{:S(2)}) copy-start(f32[1024,128]{1,0:T(8,128)} %get-tuple-element.113) | copy-start | bytes 1572868
  167.0 53.8 %all-to-all-start.3 = ((bf16[8,128,256]{1,2,0:T(8,128)(2,1)}), bf16[8,128,256]{1,2,0:T(8,128)(2,1)S(1)}, u32[]{:S(2)}, u32[]{:S(2)}) async-start(bf16[8,128,256]{1,2,0:T(8,128)(2,1)} %copy_bitcast_fusion.4), calls=%async_computation.3 | async-start | bytes 1048576 | tf_op jit(solution)/shard_map/all_to_all | solution.py:164
  219.4 8.3 %copy-start.22 = (f32[1024,128]{1,0:T(8,128)S(1)}, f32[1024,128]{1,0:T(8,128)}, u32[]{:S(2)}) copy-start(f32[1024,128]{1,0:T(8,128)} %get-tuple-element.116) | copy-start | bytes 1572868
  219.4 8.5 %copy-start.19 = (f32[1024,128]{1,0:T(8,128)S(1)}, f32[1024,128]{1,0:T(8,128)}, u32[]{:S(2)}) copy-start(f32[1024,128]{1,0:T(8,128)} %get-tuple-element.115) | copy-start | bytes 1572868
  220.8 25.0 %all-to-all-start.4 = ((bf16[8,128,256]{1,2,0:T(8,128)(2,1)}), bf16[8,128,256]{1,2,0:T(8,128)(2,1)S(1)}, u32[]{:S(2)}, u32[]{:S(2)}) async-start(bf16[8,128,256]{1,2,0:T(8,128)(2,1)} %copy_bitcast_fusion.3), calls=%async_computation.4 | async-start | bytes 1048576 | tf_op jit(solution)/shard_map/all_to_all | solution.py:165
  245.8 21.4 %all-to-all-start.5 = ((bf16[8,128,256]{1,2,0:T(8,128)(2,1)}), bf16[8,128,256]{1,2,0:T(8,128)(2,1)S(1)}, u32[]{:S(2)}, u32[]{:S(2)}) async-start(bf16[8,128,256]{1,2,0:T(8,128)(2,1)} %copy_bitcast_fusion.2), calls=%async_computation.5 | async-start | bytes 1048576 | tf_op jit(solution)/shard_map/all_to_all | solution.py:166
  (31 other events, 66.9 us)
Sparse Core Ops, SparseCore 0:
  63.4 84.5 all-gather.4
